TPU v7x, 32 devices: a whole 2x2x4 slice. The times are simulated.
32 devices in a mesh: tm: 8 (over y, x, core), tile: 4 (over z).
Axes of the slice: x: 2, y: 2, z: 4, core: 2. Of those that a mesh axis runs over, the one named last changes fastest.
Arguments:
- velocity_u: float32 [384, 2, 16, 1024], P('tm', None, None, 'tile'), may hold values from -12 to 12
- velocity_v: float32 [384, 2, 16, 1024], P('tm', None, None, 'tile'), may hold values from -12 to 12
- land_sea: int32 [16, 1024], P(None, 'tile'), may hold values 0 or 1
- bottom_level: int32 [16, 1024], P(None, 'tile'), may hold values from 0 to 2
- spacing_x: float32 [16, 1024], P(None, 'tile'), may hold values from 0.5 to 2
- spacing_y: float32 [16, 1024], P(None, 'tile'), may hold values from 0.5 to 2
Outputs:
- conversion_maps: bfloat16 [384, 2, 16, 1024], P('tm', None, None, 'tile')
- mean_map: float32 [2, 16, 1024], P(None, None, 'tile')
All inputs are finite; a program needn't handle non-finite values. No bound on the sum of `land_sea` on one device may be relied on, other than what follows from the above.
Results may differ from a plain program's by a relative error of at most 0.001.
Values sent between devices are 32-bit elements; how exact they have to be, the bound alone decides.
A program may use at most 64 MiB of HBM per device.

v0:
```python
import jax
import jax.numpy as jnp
from jax import lax
from jax.sharding import PartitionSpec as P

HALF = 24
SNAPS = 48
cutoff_freq = 1.0 / 40.0


def extended(x, sides, width):
    for axis, dim in sides:
        size, length = (lax.axis_size(axis), x.shape[dim])
        up = [(i, (i + 1) % size) for i in range(size - 1)]
        down = [(j, i) for i, j in up]
        last = lax.slice_in_dim(x, length - width, length, axis=dim)
        first = lax.slice_in_dim(x, 0, width, axis=dim)
        before = lax.ppermute(last, axis, up)
        after = lax.ppermute(first, axis, down)
        x = jnp.concatenate([before, x, after], axis=dim)
    return x


def band_matrix(count):
    out_rows = jnp.arange(count, dtype=jnp.int32)[:, None]
    in_cols = jnp.arange(count + 2 * HALF, dtype=jnp.int32)[None, :]
    offset = (in_cols - out_rows - HALF).astype(jnp.float32)
    weights = 2.0 * cutoff_freq * jnp.sinc(2.0 * cutoff_freq * offset) * jnp.sinc(offset / HALF)
    return jnp.where(jnp.abs(offset) <= HALF, weights, jnp.zeros_like(weights))


def lowpass(padded, validity, blocks, block):
    matrix = band_matrix(block)

    def one_block(block_id):
        start = block_id * block
        window = lax.dynamic_slice_in_dim(padded, start, block + 2 * HALF, 0)
        valid_part = lax.dynamic_slice_in_dim(validity, start, block + 2 * HALF, 0)
        weighted = jnp.dot(
            matrix, window, precision=lax.Precision.HIGHEST, preferred_element_type=jnp.float32
        )
        weight_sum = jnp.dot(
            matrix, valid_part, precision=lax.Precision.HIGHEST, preferred_element_type=jnp.float32
        )
        return weighted / weight_sum[:, None]

    result = lax.map(one_block, jnp.arange(blocks, dtype=jnp.int32))
    return result.reshape(blocks * block, padded.shape[1])


def wet_cells(land_sea, bottom_level, levels):
    level_ids = jnp.arange(levels, dtype=jnp.int32)[:, None, None]
    return ((land_sea[None] == 1) & (level_ids < bottom_level[None])).astype(jnp.float32)


def filter_series(series):
    length = series.shape[0]
    flattened = series.reshape(length, -1)
    padded = jnp.pad(flattened, ((HALF, HALF), (0, 0)))
    validity = jnp.pad(jnp.ones((length,), jnp.float32), (HALF, HALF))
    return lowpass(padded, validity, length // SNAPS, SNAPS).reshape(series.shape)


def shards(velocity_u, velocity_v, land_sea, bottom_level, spacing_x, spacing_y):
    block_len = velocity_u.shape[0]
    total_len = block_len * lax.axis_size("tm")
    stacked = jnp.stack([velocity_u, velocity_v], axis=1)
    full_shape = stacked.shape
    flat_cells = stacked.reshape(block_len, 2, -1)
    series_mean = filter_series(
        lax.all_to_all(flat_cells, "tm", split_axis=2, concat_axis=0, tiled=True)
    )
    mean_flat = lax.all_to_all(series_mean, "tm", split_axis=0, concat_axis=2, tiled=True)
    mean_flow = mean_flat.reshape(full_shape)
    eddies = stacked - mean_flow
    wet_mask = wet_cells(land_sea, bottom_level, full_shape[2])
    masked = mean_flow * wet_mask[None, None]
    edge_cols = jnp.concatenate([masked[..., :1], masked[..., -1:]], axis=4)
    edge_ext = extended(edge_cols, (("tile", 4),), 1)
    left_col = edge_ext[..., :1]
    right_col = edge_ext[..., 3:4]
    ahead = jnp.concatenate([masked[..., 1:], right_col], axis=4)
    behind = jnp.concatenate([left_col, masked[..., :-1]], axis=4)
    grad_x = (ahead - behind) * (0.5 / spacing_x)
    row_padded = jnp.pad(masked, ((0, 0), (0, 0), (0, 0), (1, 1), (0, 0)))
    grad_y = (row_padded[..., 2:, :] - row_padded[..., :-2, :]) * (0.5 / spacing_y)
    eddy_u = eddies[:, 0]
    eddy_v = eddies[:, 1]
    total = (
        eddy_u * eddy_u * grad_x[:, 0]
        + eddy_u * eddy_v * (grad_y[:, 0] + grad_x[:, 1])
        + eddy_v * eddy_v * grad_y[:, 1]
    )
    conversion = -wet_mask[None] * total
    summed = lax.psum(jnp.sum(conversion, axis=0), "tm")
    return (conversion.astype(jnp.bfloat16), summed / total_len)


def solution(mesh):
    in_specs = (
        P("tm", None, None, "tile"),
        P("tm", None, None, "tile"),
        P(None, "tile"),
        P(None, "tile"),
        P(None, "tile"),
        P(None, "tile"),
    )
    out_specs = (P("tm", None, None, "tile"), P(None, None, "tile"))
    return jax.shard_map(shards, mesh=mesh, in_specs=in_specs, out_specs=out_specs, check_vma=False)
```

profile of v0, /device:TPU:0, one launch (start us, length us, event | category | flops | bytes accessed | tf_op | source)
XLA Modules:
  0.0 262.7 jit_solution(6098952019784487532)
XLA Ops:
  0.6 2.7 %stack.18 = f32[48,1,8192]{2,0,1:T(8,128)} reshape(f32[48,2,16,256]{3,2,1,0:T(8,128)} %param.9) | data formatting | bytes 3145728 | tf_op jit(solution)/shard_map/stack | solution.py:67
  6.9 8.0 %copy.21 = f32[48,2,8192]{0,1,2:T(2,128)} copy(f32[48,2,8192]{2,0,1:T(8,128)S(1)} %pad_maximum_fusion) | data formatting | bytes 6291456 | tf_op jit(solution)/shard_map/stack | solution.py:67
  14.9 16.2 %reshape.50 = f32[8,1,98304]{2,1,0:T(1,128)} reshape(f32[8192,2,48]{2,1,0:T(2,128)} %bitcast.49) | data formatting | bytes 6291456
  31.0 5.4 %all-to-all-start = ((f32[8,1,98304]{2,1,0:T(1,128)}), f32[8,1,98304]{2,1,0:T(1,128)S(1)}, u32[]{:S(2)}, u32[]{:S(2)}) async-start(f32[8,1,98304]{2,1,0:T(1,128)} %reshape.50), calls=%async_computation | async-start | bytes 6291456 | tf_op jit(solution)/shard_map/all_to_all | solution.py:71
  37.2 36.8 %all-to-all-done = f32[8,1,98304]{2,1,0:T(1,128)S(1)} async-done(((f32[8,1,98304]{2,1,0:T(1,128)}), f32[8,1,98304]{2,1,0:T(1,128)S(1)}, u32[]{:S(2)}, u32[]{:S(2)}) %all-to-all-start) | async-done | bytes 3145760 | tf_op jit(solution)/shard_map/all_to_all | solution.py:71
  74.6 11.2 %reduce = f32[8,98304]{1,0:T(8,128)} reduce(f32[8,1,98304]{2,1,0:T(1,128)S(1)} %all-to-all-done, f32[]{:T(128)} %broadcast.65), dimensions={1}, to_apply=%all_to_all.22.reduce_sub_computation | reduce | bytes 6291460 | tf_op jit(solution)/shard_map/all_to_all | solution.py:71
  85.8 19.3 %reshape.51 = f32[8192,2,48]{2,1,0:T(2,128)} reshape(f32[8,98304]{1,0:T(8,128)} %reduce) | data formatting | bytes 6291456
  105.1 7.0 %copy.30 = f32[48,2,8,1024]{3,2,0,1:T(8,128)S(1)} copy(f32[48,2,8,1024]{0,1,3,2:T(2,128)} %bitcast.50) | data formatting | bytes 6291456 | tf_op jit(solution)/shard_map/all_to_all | solution.py:71
  112.1 2.4 copy.23
  116.3 34.3 %while.11 = (s32[]{:T(128)}, f32[8,48,2048]{2,1,0:T(8,128)}, s32[8]{0:T(128)S(1)}, f32[432,2048]{1,0:T(8,128)S(1)}, f32[48,96]{1,0:T(8,128)}, /*index=5*/f32[432...) while((s32[]{:T(128)}, f32[8,48,2048]{2,1,0:T(8,128)}, s32[8]{0:T(128)S(1)}, ...), condition=%wide.region_1.3_spmd.clone, body=%wide.region_0.2_spmd.clone.sunk | while | flops 113399816 | bytes 1224551 | solution.py:47
  118.5 2.1 fusion.59
  122.9 2.1 fusion.59
  127.1 2.1 fusion.59
  131.4 2.1 fusion.59
  140.0 2.1 fusion.59
  144.3 2.1 fusion.59
  150.6 5.6 %reshape_reshape.3 = f32[384,2,1024]{2,1,0:T(2,128)} reshape(f32[8,48,2048]{2,1,0:T(8,128)} %get-tuple-element.38) | data formatting | bytes 6291456 | tf_op jit(solution)/shard_map/reshape;reshape | solution.py:61
  156.2 4.0 %all-to-all-start.1 = ((f32[384,2,1024]{2,1,0:T(2,128)}), f32[384,2,1024]{2,1,0:T(2,128)S(1)}, u32[]{:S(2)}, u32[]{:S(2)}) async-start(f32[384,2,1024]{2,1,0:T(2,128)} %reshape_reshape.3), calls=%async_computation.1 | async-start | bytes 6291456 | tf_op jit(solution)/shard_map/all_to_all | solution.py:73
  160.3 37.7 %all-to-all-done.1 = f32[384,2,1024]{2,1,0:T(2,128)S(1)} async-done(((f32[384,2,1024]{2,1,0:T(2,128)}), f32[384,2,1024]{2,1,0:T(2,128)S(1)}, u32[]{:S(2)}, u32[]{:S(2)}) %all-to-all-start.1) | async-done | bytes 3145760 | tf_op jit(solution)/shard_map/all_to_all | solution.py:73
  200.8 2.6 reshape.47
  203.4 5.7 %maximum_subtract_fusion = (f32[48,2,2,16,256]{4,3,2,1,0:T(8,128)}, f32[48,2,2,16,256]{4,3,2,1,0:T(8,128)S(1)}) fusion(f32[48,2,2,16,256]{4,3,2,1,0:T(8,128)} %reshape.47, f32[48,1,2,16,256]{4,3,2,1,0:T(8,128)} %bitcast.55, f32[48,1,2,16,256]{4,3,2,1,0:T(8,128)} %bitcast.56, f32[2,16,256]{2,1,0:T(8,128)S(1)} %fusion.15), kind=kLoop, calls=%fused_computation.12 | loop fusion | flops 2359296 | bytes 12615680 | tf_op jit(solution)/shard_map/sub | solution.py:75
  209.1 3.7 %fusion.47 = (f32[48,2,2,16,255]{4,3,2,1,0:T(8,128)}, f32[48,2,2,16,255]{4,3,2,1,0:T(8,128)}) fusion(f32[48,2,2,16,256]{4,3,2,1,0:T(8,128)S(1)} %get-tuple-element.70), kind=kLoop, calls=%fused_computation.85 | loop fusion | bytes 12533760 | tf_op jit(solution)/shard_map/slice | solution.py:83
  212.8 2.3 fusion.46
  215.1 2.2 copy.26
  218.6 2.2 copy.28
  220.8 4.7 %collective-permute-start.1 = (f32[48,2,2,16,1]{0,3,4,2,1:T(8,128)S(1)}, f32[48,2,2,16,1]{0,3,4,2,1:T(8,128)S(1)}, u32[]{:S(2)}, u32[]{:S(2)}) collective-permute-start(f32[48,2,2,16,1]{0,3,4,2,1:T(8,128)S(1)} %copy.28), channel_id=1, source_target_pairs={{0,1},{1,2},{2,3},{4,5},{5,6},{6,7},{8,9},{9,10},{10,11},{12,13},{... | collective-permute-start | bytes 36872 | tf_op jit(solution)/shard_map/ppermute | solution.py:18
  225.5 2.4 fusion.7
  228.0 2.4 copy.27
  230.3 2.4 copy.29
  232.7 4.3 %fusion.8 = f32[48,2,2,16,256]{4,3,2,1,0:T(8,128)S(1)} fusion(f32[48,2,2,16,1]{4,3,2,1,0:T(8,128)} %copy.27, f32[48,2,2,16,255]{4,3,2,1,0:T(8,128)} %get-tuple-element.74, f32[48,2,2,16,255]{4,3,2,1,0:T(8,128)S(1)} %copy-done.2, f32[48,2,2,16,1]{4,3,2,1,0:T(8,128)} %copy.29, f32[16,256]{1,0:T(8,128)S(1)} %broadcast_divide_fusion.1), kind=kLoop, calls=%fused_computation.15 | loop fusion | flops 3145728 | bytes 9453568 | tf_op jit(solution)/shard_map/mul | solution.py:84
  237.4 2.1 fusion.44
  239.5 22.3 %psum.7 = f32[2,16,256]{2,1,0:T(8,128)S(1)} all-reduce(f32[2,16,256]{2,1,0:T(8,128)S(1)} %get-tuple-element.67), channel_id=1, replica_groups=mesh['tm'=8,'tile'=4] {'tm'}, use_global_device_ids=true, to_apply=%region_3.5 | all-reduce | flops 8192 | bytes 65536 | tf_op jit(solution)/shard_map/psum | solution.py:95
  (55 shorter events, 28.3 us)
Async XLA Ops:
  0.6 2.7 %copy-start.3 = (f32[48,2,16,256]{3,2,1,0:T(8,128)S(1)}, f32[48,2,16,256]{3,2,1,0:T(8,128)}, u32[]{:S(2)}) copy-start(f32[48,2,16,256]{3,2,1,0:T(8,128)} %param.10) | copy-start | bytes 4718596
  31.0 43.1 %all-to-all-start = ((f32[8,1,98304]{2,1,0:T(1,128)}), f32[8,1,98304]{2,1,0:T(1,128)S(1)}, u32[]{:S(2)}, u32[]{:S(2)}) async-start(f32[8,1,98304]{2,1,0:T(1,128)} %reshape.50), calls=%async_computation | async-start | bytes 6291456 | tf_op jit(solution)/shard_map/all_to_all | solution.py:71
  156.2 4.0 %copy-start.5 = (s32[16,256]{1,0:T(8,128)S(1)}, s32[16,256]{1,0:T(8,128)}, u32[]{:S(2)}) copy-start(s32[16,256]{1,0:T(8,128)} %param.11) | copy-start | bytes 49156
  156.2 4.0 %copy-start.6 = (f32[16,256]{1,0:T(8,128)S(1)}, f32[16,256]{1,0:T(8,128)}, u32[]{:S(2)}) copy-start(f32[16,256]{1,0:T(8,128)} %param.13) | copy-start | bytes 49156
  156.2 4.0 %copy-start.7 = (f32[16,256]{1,0:T(8,128)S(1)}, f32[16,256]{1,0:T(8,128)}, u32[]{:S(2)}) copy-start(f32[16,256]{1,0:T(8,128)} %param.14) | copy-start | bytes 49156
  156.2 4.1 %copy-start.4 = (s32[16,256]{1,0:T(8,128)S(1)}, s32[16,256]{1,0:T(8,128)}, u32[]{:S(2)}) copy-start(s32[16,256]{1,0:T(8,128)} %param.12) | copy-start | bytes 49156
  156.2 41.8 %all-to-all-start.1 = ((f32[384,2,1024]{2,1,0:T(2,128)}), f32[384,2,1024]{2,1,0:T(2,128)S(1)}, u32[]{:S(2)}, u32[]{:S(2)}) async-start(f32[384,2,1024]{2,1,0:T(2,128)} %reshape_reshape.3), calls=%async_computation.1 | async-start | bytes 6291456 | tf_op jit(solution)/shard_map/all_to_all | solution.py:73
  217.3 10.7 %collective-permute-start = (f32[48,2,2,16,1]{0,3,4,2,1:T(8,128)S(1)}, f32[48,2,2,16,1]{0,3,4,2,1:T(8,128)S(1)}, u32[]{:S(2)}, u32[]{:S(2)}) collective-permute-start(f32[48,2,2,16,1]{0,3,4,2,1:T(8,128)S(1)} %copy.26), channel_id=1, source_target_pairs={{1,0},{2,1},{3,2},{5,4},{6,5},{7,6},{9,8},{10,9},{11,10},{13,12},{... | collective-permute-start | bytes 36872 | tf_op jit(solution)/shard_map/ppermute | solution.py:19
  220.8 9.6 %collective-permute-start.1 = (f32[48,2,2,16,1]{0,3,4,2,1:T(8,128)S(1)}, f32[48,2,2,16,1]{0,3,4,2,1:T(8,128)S(1)}, u32[]{:S(2)}, u32[]{:S(2)}) collective-permute-start(f32[48,2,2,16,1]{0,3,4,2,1:T(8,128)S(1)} %copy.28), channel_id=1, source_target_pairs={{0,1},{1,2},{2,3},{4,5},{5,6},{6,7},{8,9},{9,10},{10,11},{12,13},{... | collective-permute-start | bytes 36872 | tf_op jit(solution)/shard_map/ppermute | solution.py:18
  228.0 4.7 %copy-start.2 = (f32[48,2,2,16,255]{4,3,2,1,0:T(8,128)S(1)}, f32[48,2,2,16,255]{4,3,2,1,0:T(8,128)}, u32[]{:S(2)}) copy-start(f32[48,2,2,16,255]{4,3,2,1,0:T(8,128)} %get-tuple-element.73) | copy-start | bytes 9400324
  232.7 4.3 %copy-start = (f32[48,2,2,16,256]{4,3,2,1,0:T(8,128)S(1)}, f32[48,2,2,16,256]{4,3,2,1,0:T(8,128)}, u32[]{:S(2)}) copy-start(f32[48,2,2,16,256]{4,3,2,1,0:T(8,128)} %fusion.7) | copy-start | bytes 9437188
  232.7 4.7 %copy-start.1 = (f32[48,2,2,16,256]{4,3,2,1,0:T(8,128)S(1)}, f32[48,2,2,16,256]{4,3,2,1,0:T(8,128)}, u32[]{:S(2)}) copy-start(f32[48,2,2,16,256]{4,3,2,1,0:T(8,128)} %get-tuple-element.69) | copy-start | bytes 9437188
where the time goes:
time: 267 us; the launch traced here: 263 us
  local copies, waits for them, and re-layouts  90.8 us (34%)
  waiting for transfers between devices  74.5 us (28%)
  other arithmetic  29.2 us (11%)
  matrix products  24.2 us (9%)
  blocking collectives  22.3 us (8%)
  starting transfers between devices  15.4 us (6%)
  loops' own time  5.18 us (2%)
    all_to_all x1, waiting for transfers between devices, shards(): lax.all_to_all(series_mean, 'tm', split_axis=0, concat_axis=2, tiled=True)  37.7 us
    unnamed x19, local copies, waits for them, and re-layouts  37.3 us
    all_to_all x1, waiting for transfers between devices, shards(): lax.all_to_all(flat_cells, 'tm', split_axis=2, concat_axis=0, tiled=True)  36.8 us
    psum x1, blocking collectives, shards(): summed = lax.psum(jnp.sum(conversion, axis=0), 'tm')  22.3 us
    dot_general x8, matrix products, one_block(): jnp.dot(matrix, window, precision=lax.Precision.HIGHEST, preferred_elemen...  16.8 us
    another operation x3, local copies, waits for them, and re-layouts, shards(): stacked = jnp.stack([velocity_u, velocity_v], axis=1)  12.1 us
    all_to_all x1, other arithmetic, shards(): lax.all_to_all(flat_cells, 'tm', split_axis=2, concat_axis=0, tiled=True)  11.2 us
    all_to_all x3, local copies, waits for them, and re-layouts, shards(): lax.all_to_all(flat_cells, 'tm', split_axis=2, concat_axis=0, tiled=True)  9.91 us
  transfers between devices with their start and end apart: 4, of which 2 were waited for; matrix products, arithmetic and copies ran while one was open for 3% of the time, Pallas kernels for 0%

commit v1 on v0

--- a/solution.py
+++ b/solution.py
@@ -6,6 +6,29 @@
 HALF = 24
 SNAPS = 48
 cutoff_freq = 1.0 / 40.0
+
+
+def in_blocks(shard, dim, devices):
+    shape = shard.shape
+    blocks = shard.reshape(*shape[:dim], devices, shape[dim] // devices, *shape[dim + 1 :])
+    return jnp.moveaxis(blocks, dim, 0)
+
+
+def in_order(parts, dim):
+    shape = list(parts.shape[1:])
+    shape[dim] *= parts.shape[0]
+    return jnp.moveaxis(parts, 0, dim).reshape(shape)
+
+
+def swapped_with_each(x, axis, split_dim, concat_dim):
+    size, place = (lax.axis_size(axis), lax.axis_index(axis))
+    pieces = in_blocks(x, split_dim, size)
+    outs = [pieces[place]]
+    for step in range(1, size):
+        sent = pieces[place ^ step]
+        outs.append(lax.ppermute(sent, axis, [(i, i ^ step) for i in range(size)]))
+    pieces = jnp.stack(outs)[place ^ jnp.arange(size)]
+    return in_order(pieces, concat_dim)
 
 
 def extended(x, sides, width):
@@ -67,9 +90,7 @@
     stacked = jnp.stack([velocity_u, velocity_v], axis=1)
     full_shape = stacked.shape
     flat_cells = stacked.reshape(block_len, 2, -1)
-    series_mean = filter_series(
-        lax.all_to_all(flat_cells, "tm", split_axis=2, concat_axis=0, tiled=True)
-    )
+    series_mean = filter_series(swapped_with_each(flat_cells, "tm", 2, 0))
     mean_flat = lax.all_to_all(series_mean, "tm", split_axis=0, concat_axis=2, tiled=True)
     mean_flow = mean_flat.reshape(full_shape)
     eddies = stacked - mean_flow

time: 267 us -> 210 us (0.79)
  local copies, waits for them, and re-layouts: 90.8 us -> 60.9 us
  waiting for transfers between devices: 74.5 us -> 59.1 us
  other arithmetic: 29.2 us -> 15.9 us
  starting transfers between devices: 15.4 us -> 19.5 us
    all_to_all x1 -> x0, waiting for transfers between devices: 36.8 us -> none  [shards(): lax.all_to_all(flat_cells, 'tm', split_axis=2, concat_axis=0, tiled=True)]
    unnamed x19 -> x23, local copies, waits for them, and re-layouts: 37.3 us -> 14.6 us
    ppermute x0 -> x7, waiting for transfers between devices: none -> 21.4 us  [swapped_with_each(): outs.append(lax.ppermute(sent, axis, [(i, i ^ step) for i in range(size)]))]
    all_to_all x1 -> x0, other arithmetic: 11.2 us -> none  [shards(): lax.all_to_all(flat_cells, 'tm', split_axis=2, concat_axis=0, tiled=True)]
    all_to_all x3 -> x0, local copies, waits for them, and re-layouts: 9.91 us -> none  [shards(): lax.all_to_all(flat_cells, 'tm', split_axis=2, concat_axis=0, tiled=True)]
    ppermute x0 -> x7, starting transfers between devices: none -> 9.24 us  [swapped_with_each(): outs.append(lax.ppermute(sent, axis, [(i, i ^ step) for i in range(size)]))]
    all_to_all x1 -> x0, starting transfers between devices: 5.44 us -> none  [shards(): lax.all_to_all(flat_cells, 'tm', split_axis=2, concat_axis=0, tiled=True)]
    gather x0 -> x2, local copies, waits for them, and re-layouts: none -> 5.06 us  [swapped_with_each(): pieces = jnp.stack(outs)[place ^ jnp.arange(size)]]
  transfers between devices with their start and end apart: 4 -> 10, of which waited for: 2 -> 4; matrix products, arithmetic and copies ran while one was open for 3% -> 9% of each run, Pallas kernels for 0% -> 0%
where the time goes in v1:
time: 210 us; the launch traced here: 208 us
  local copies, waits for them, and re-layouts  60.9 us (29%)
  waiting for transfers between devices  59.1 us (28%)
  matrix products  24.1 us (11%)
  blocking collectives  22.3 us (11%)
  starting transfers between devices  19.5 us (9%)
  other arithmetic  15.9 us (8%)
  loops' own time  5.28 us (3%)
    all_to_all x1, waiting for transfers between devices, shards(): lax.all_to_all(series_mean, 'tm', split_axis=0, concat_axis=2, tiled=True)  37.8 us
    psum x1, blocking collectives, shards(): summed = lax.psum(jnp.sum(conversion, axis=0), 'tm')  22.3 us
    ppermute x7, waiting for transfers between devices, swapped_with_each(): outs.append(lax.ppermute(sent, axis, [(i, i ^ step) for i in range(size)]))  21.4 us
    dot_general x8, matrix products, one_block(): jnp.dot(matrix, window, precision=lax.Precision.HIGHEST, preferred_elemen...  16.7 us
    unnamed x23, local copies, waits for them, and re-layouts  14.6 us
    ppermute x7, starting transfers between devices, swapped_with_each(): outs.append(lax.ppermute(sent, axis, [(i, i ^ step) for i in range(size)]))  9.24 us
    another operation x3, local copies, waits for them, and re-layouts, shards(): stacked = jnp.stack([velocity_u, velocity_v], axis=1)  7.73 us
    dot_general x8, matrix products, one_block(): jnp.dot(matrix, valid_part, precision=lax.Precision.HIGHEST, preferred_el...  7.47 us
  transfers between devices with their start and end apart: 10, of which 4 were waited for; matrix products, arithmetic and copies ran while one was open for 9% of the time, Pallas kernels for 0%

profile of v1, /device:TPU:0, one launch (start us, length us, event | category | flops | bytes accessed | tf_op | source)
XLA Modules:
  0.0 208.1 jit_solution(14855600303451213229)
XLA Ops:
  0.7 2.7 %stack.42 = f32[48,1,8,1024]{3,2,0,1:T(8,128)} reshape(f32[48,2,16,256]{3,2,1,0:T(8,128)} %param.9) | data formatting | bytes 3145728 | tf_op jit(solution)/shard_map/stack | solution.py:90
  3.4 2.3 %copy_dynamic-update-slice_fusion.1 = f32[48,2,8,1024]{3,0,1,2:T(8,128)S(1)} fusion(f32[48,1,8,1024]{3,2,0,1:T(8,128)} %stack.42), kind=kLoop, calls=%fused_computation.25 | loop fusion | bytes 3145728
  5.7 2.7 %stack.43 = f32[48,1,8,1024]{3,2,0,1:T(8,128)} reshape(f32[48,2,16,256]{3,2,1,0:T(8,128)} %param.10) | data formatting | bytes 3145728 | tf_op jit(solution)/shard_map/stack | solution.py:90
  8.4 2.3 %copy_dynamic-update-slice_fusion = f32[48,2,8,1024]{3,0,1,2:T(8,128)S(1)} fusion(f32[48,2,8,1024]{3,0,1,2:T(8,128)S(1)} %copy_dynamic-update-slice_fusion.1, f32[48,1,8,1024]{3,2,0,1:T(8,128)} %stack.43), kind=kLoop, calls=%fused_computation.24 | loop fusion | bytes 3145728 | tf_op jit(solution)/shard_map/stack | solution.py:90
  12.6 2.5 %collective-permute-start.1 = (f32[48,2,1024]{2,0,1:T(8,128)}, f32[48,2,1024]{2,0,1:T(8,128)}, u32[]{:S(2)}, u32[]{:S(2)}) collective-permute-start(f32[48,2,1024]{2,0,1:T(8,128)} %get-tuple-element.80), channel_id=1, source_target_pairs={{0,8},{4,12},{8,0},{12,4},{16,24},{20,28},{24,16},{28,20},{1,9},{5... | collective-permute-start | bytes 1179656 | tf_op jit(solution)/shard_map/ppermute | solution.py:29
  18.6 2.6 %collective-permute-start.5 = (f32[48,2,1024]{2,0,1:T(8,128)}, f32[48,2,1024]{2,0,1:T(8,128)S(1)}, u32[]{:S(2)}, u32[]{:S(2)}) collective-permute-start(f32[48,2,1024]{2,0,1:T(8,128)} %get-tuple-element.76), channel_id=1, source_target_pairs={{0,24},{4,28},{8,16},{12,20},{16,8},{20,12},{24,0},{28,4},{1,25},{... | collective-permute-start | bytes 1179656 | tf_op jit(solution)/shard_map/ppermute | solution.py:29
  22.9 2.5 %collective-permute-done.1 = f32[48,2,1024]{2,0,1:T(8,128)} collective-permute-done((f32[48,2,1024]{2,0,1:T(8,128)}, f32[48,2,1024]{2,0,1:T(8,128)}, u32[]{:S(2)}, u32[]{:S(2)}) %collective-permute-start.1) | collective-permute-done | bytes 393248 | tf_op jit(solution)/shard_map/ppermute | solution.py:29
  29.0 4.5 %collective-permute-done.2 = f32[48,2,1024]{2,0,1:T(8,128)} collective-permute-done((f32[48,2,1024]{2,0,1:T(8,128)}, f32[48,2,1024]{2,0,1:T(8,128)}, u32[]{:S(2)}, u32[]{:S(2)}) %collective-permute-start.2) | collective-permute-done | bytes 393248 | tf_op jit(solution)/shard_map/ppermute | solution.py:29
  37.0 14.4 %collective-permute-done.4 = f32[48,2,1024]{2,0,1:T(8,128)} collective-permute-done((f32[48,2,1024]{2,0,1:T(8,128)}, f32[48,2,1024]{2,0,1:T(8,128)}, u32[]{:S(2)}, u32[]{:S(2)}) %collective-permute-start.4) | collective-permute-done | bytes 393248 | tf_op jit(solution)/shard_map/ppermute | solution.py:29
  54.8 2.6 %gather_fusion = f32[8,48,2,1024]{3,1,2,0:T(8,128)S(1)} fusion(f32[8,48,2,1024]{3,1,2,0:T(8,128)} %bitcast_dynamic-update-slice_fusion, s32[1024]{0:T(1024)S(1)} %pad_clamp_fusion), kind=kCustom, calls=%fused_computation | custom fusion | bytes 6291488 | tf_op jit(solution)/shard_map/gather | solution.py:30
  57.5 2.4 %copy.17 = f32[8,48,2,1024]{3,2,1,0:T(2,128)S(1)} copy(f32[8,48,2,1024]{3,1,2,0:T(8,128)S(1)} %gather_fusion) | data formatting | bytes 6291456 | tf_op jit(solution)/shard_map/gather | solution.py:30
  61.7 34.1 %while.11 = (s32[]{:T(128)}, f32[8,48,2048]{2,1,0:T(8,128)}, s32[8]{0:T(128)S(1)}, f32[432,2048]{1,0:T(8,128)S(1)}, f32[48,96]{1,0:T(8,128)}, /*index=5*/f32[432...) while((s32[]{:T(128)}, f32[8,48,2048]{2,1,0:T(8,128)}, s32[8]{0:T(128)S(1)}, ...), condition=%wide.region_1.3_spmd.clone, body=%wide.region_0.2_spmd.clone.sunk | while | flops 113399816 | bytes 1224551 | solution.py:70
  63.9 2.1 %fusion.60 = f32[8,48,2048]{2,1,0:T(8,128)} fusion(f32[8,48,2048]{2,1,0:T(8,128)} %get-tuple-element.132, s32[]{:T(128)} %get-tuple-element.131, f32[48,96]{1,0:T(8,128)} %get-tuple-element.145, f32[432,2048]{1,0:T(8,128)S(1)} %get-tuple-element.144, s32[]{:T(128)S(6)} %select_n.193, f32[48]{0:T(128)S(1)} %convolution_bitcast_fusion.2), kind=kOutput, calls=%fused_computation.3.clone.1 | convolution fusion | flops 113344512 | bytes 1205252 | tf_op jit(solution)/shard_map/while/body/eval_jaxpr/dot_general | solution.py:62
  72.4 2.1 %fusion.60 = f32[8,48,2048]{2,1,0:T(8,128)} fusion(f32[8,48,2048]{2,1,0:T(8,128)} %get-tuple-element.132, s32[]{:T(128)} %get-tuple-element.131, f32[48,96]{1,0:T(8,128)} %get-tuple-element.145, f32[432,2048]{1,0:T(8,128)S(1)} %get-tuple-element.144, s32[]{:T(128)S(6)} %select_n.193, f32[48]{0:T(128)S(1)} %convolution_bitcast_fusion.2), kind=kOutput, calls=%fused_computation.3.clone.1 | convolution fusion | flops 113344512 | bytes 1205252 | tf_op jit(solution)/shard_map/while/body/eval_jaxpr/dot_general | solution.py:62
  80.9 2.1 %fusion.60 = f32[8,48,2048]{2,1,0:T(8,128)} fusion(f32[8,48,2048]{2,1,0:T(8,128)} %get-tuple-element.132, s32[]{:T(128)} %get-tuple-element.131, f32[48,96]{1,0:T(8,128)} %get-tuple-element.145, f32[432,2048]{1,0:T(8,128)S(1)} %get-tuple-element.144, s32[]{:T(128)S(6)} %select_n.193, f32[48]{0:T(128)S(1)} %convolution_bitcast_fusion.2), kind=kOutput, calls=%fused_computation.3.clone.1 | convolution fusion | flops 113344512 | bytes 1205252 | tf_op jit(solution)/shard_map/while/body/eval_jaxpr/dot_general | solution.py:62
  93.7 2.1 %fusion.60 = f32[8,48,2048]{2,1,0:T(8,128)} fusion(f32[8,48,2048]{2,1,0:T(8,128)} %get-tuple-element.132, s32[]{:T(128)} %get-tuple-element.131, f32[48,96]{1,0:T(8,128)} %get-tuple-element.145, f32[432,2048]{1,0:T(8,128)S(1)} %get-tuple-element.144, s32[]{:T(128)S(6)} %select_n.193, f32[48]{0:T(128)S(1)} %convolution_bitcast_fusion.2), kind=kOutput, calls=%fused_computation.3.clone.1 | convolution fusion | flops 113344512 | bytes 1205252 | tf_op jit(solution)/shard_map/while/body/eval_jaxpr/dot_general | solution.py:62
  95.8 5.6 %reshape_reshape.8 = f32[384,2,1024]{2,1,0:T(2,128)} reshape(f32[8,48,2048]{2,1,0:T(8,128)} %get-tuple-element.38) | data formatting | bytes 6291456 | tf_op jit(solution)/shard_map/reshape;reshape | solution.py:84
  101.5 4.3 %all-to-all-start = ((f32[384,2,1024]{2,1,0:T(2,128)}), f32[384,2,1024]{2,1,0:T(2,128)S(1)}, u32[]{:S(2)}, u32[]{:S(2)}) async-start(f32[384,2,1024]{2,1,0:T(2,128)} %reshape_reshape.8), calls=%async_computation | async-start | bytes 6291456 | tf_op jit(solution)/shard_map/all_to_all | solution.py:94
  105.8 37.8 %all-to-all-done = f32[384,2,1024]{2,1,0:T(2,128)S(1)} async-done(((f32[384,2,1024]{2,1,0:T(2,128)}), f32[384,2,1024]{2,1,0:T(2,128)S(1)}, u32[]{:S(2)}, u32[]{:S(2)}) %all-to-all-start) | async-done | bytes 3145760 | tf_op jit(solution)/shard_map/all_to_all | solution.py:94
  146.4 2.6 %reshape.72 = f32[48,2,2,16,256]{4,3,2,1,0:T(8,128)} reshape(f32[48,2,8,1024]{3,2,1,0:T(8,128)S(1)} %copy.19) | data formatting | bytes 6291456 | tf_op jit(solution)/shard_map/reshape | solution.py:95
  149.0 5.7 %maximum_subtract_fusion = (f32[48,2,2,16,256]{4,3,2,1,0:T(8,128)}, f32[48,2,2,16,256]{4,3,2,1,0:T(8,128)S(1)}) fusion(f32[48,2,2,16,256]{4,3,2,1,0:T(8,128)} %reshape.72, f32[48,1,2,16,256]{4,3,2,1,0:T(8,128)} %bitcast.81, f32[48,1,2,16,256]{4,3,2,1,0:T(8,128)} %bitcast.80, f32[2,16,256]{2,1,0:T(8,128)S(1)} %fusion.15), kind=kLoop, calls=%fused_computation.13 | loop fusion | flops 2359296 | bytes 12615680 | tf_op jit(solution)/shard_map/sub | solution.py:96
  154.7 3.7 %fusion.48 = (f32[48,2,2,16,255]{4,3,2,1,0:T(8,128)}, f32[48,2,2,16,255]{4,3,2,1,0:T(8,128)}) fusion(f32[48,2,2,16,256]{4,3,2,1,0:T(8,128)S(1)} %get-tuple-element.70), kind=kLoop, calls=%fused_computation.105 | loop fusion | bytes 12533760 | tf_op jit(solution)/shard_map/slice | solution.py:104
  158.4 2.3 %fusion.47 = (f32[48,2,2,16,1]{4,3,2,1,0:T(8,128)}, f32[48,2,2,16,1]{4,3,2,1,0:T(8,128)}) fusion(f32[48,2,2,16,256]{4,3,2,1,0:T(8,128)S(1)} %get-tuple-element.70), kind=kLoop, calls=%fused_computation.104 | loop fusion | bytes 49152 | tf_op jit(solution)/shard_map/slice | solution.py:99
  160.7 2.2 %copy.20 = f32[48,2,2,16,1]{0,3,4,2,1:T(8,128)S(1)} copy(f32[48,2,2,16,1]{4,3,2,1,0:T(8,128)} %get-tuple-element.72) | data formatting | bytes 24576 | tf_op jit(solution)/shard_map/slice | solution.py:99
  164.2 2.2 %copy.22 = f32[48,2,2,16,1]{0,3,4,2,1:T(8,128)S(1)} copy(f32[48,2,2,16,1]{4,3,2,1,0:T(8,128)} %get-tuple-element.71) | data formatting | bytes 24576 | tf_op jit(solution)/shard_map/slice | solution.py:99
  166.4 4.8 %collective-permute-start.8 = (f32[48,2,2,16,1]{0,3,4,2,1:T(8,128)S(1)}, f32[48,2,2,16,1]{0,3,4,2,1:T(8,128)S(1)}, u32[]{:S(2)}, u32[]{:S(2)}) collective-permute-start(f32[48,2,2,16,1]{0,3,4,2,1:T(8,128)S(1)} %copy.22), channel_id=1, source_target_pairs={{0,1},{1,2},{2,3},{4,5},{5,6},{6,7},{8,9},{9,10},{10,11},{12,13},{... | collective-permute-start | bytes 36872 | tf_op jit(solution)/shard_map/ppermute | solution.py:41
  171.1 2.4 %fusion.7 = f32[48,2,2,16,256]{4,3,2,1,0:T(8,128)} fusion(f32[48,2,2,16,256]{4,3,2,1,0:T(8,128)S(1)} %get-tuple-element.70, f32[16,256]{1,0:T(8,128)S(1)} %broadcast_divide_fusion), kind=kLoop, calls=%fused_computation.12 | loop fusion | flops 1572864 | bytes 6307840 | tf_op jit(solution)/shard_map/mul | solution.py:107
  173.5 2.4 %copy.21 = f32[48,2,2,16,1]{4,3,2,1,0:T(8,128)} copy(f32[48,2,2,16,1]{0,3,4,2,1:T(8,128)S(1)} %collective-permute-done.7) | data formatting | bytes 24576 | tf_op jit(solution)/shard_map/ppermute | solution.py:42
  175.9 2.4 %copy.23 = f32[48,2,2,16,1]{4,3,2,1,0:T(8,128)} copy(f32[48,2,2,16,1]{0,3,4,2,1:T(8,128)S(1)} %collective-permute-done.8) | data formatting | bytes 24576 | tf_op jit(solution)/shard_map/ppermute | solution.py:41
  178.3 4.3 %fusion.8 = f32[48,2,2,16,256]{4,3,2,1,0:T(8,128)S(1)} fusion(f32[48,2,2,16,1]{4,3,2,1,0:T(8,128)} %copy.21, f32[48,2,2,16,255]{4,3,2,1,0:T(8,128)} %get-tuple-element.74, f32[48,2,2,16,255]{4,3,2,1,0:T(8,128)S(1)} %copy-done.2, f32[48,2,2,16,1]{4,3,2,1,0:T(8,128)} %copy.23, f32[16,256]{1,0:T(8,128)S(1)} %broadcast_divide_fusion.1), kind=kLoop, calls=%fused_computation.15 | loop fusion | flops 3145728 | bytes 9453568 | tf_op jit(solution)/shard_map/mul | solution.py:105
  183.0 2.1 %fusion.45 = (f32[2,16,256]{2,1,0:T(8,128)S(1)}, bf16[48,2,16,256]{3,2,1,0:T(8,128)(2,1)}) fusion(f32[48,2,2,16,256]{4,3,2,1,0:T(8,128)S(1)} %copy-done, f32[48,2,2,16,256]{4,3,2,1,0:T(8,128)S(1)} %fusion.8, f32[48,2,2,16,256]{4,3,2,1,0:T(8,128)S(1)} %copy-done.1, f32[2,16,256]{2,1,0:T(8,128)S(1)} %fusion.44), kind=kLoop, calls=%fused_computation.103 | loop fusion | flops 4710400 | bytes 10289152 | tf_op jit(solution)/shard_map/reduce_sum | solution.py:116
  185.2 22.3 %psum.7 = f32[2,16,256]{2,1,0:T(8,128)S(1)} all-reduce(f32[2,16,256]{2,1,0:T(8,128)S(1)} %get-tuple-element.67), channel_id=1, replica_groups=mesh['tm'=8,'tile'=4] {'tm'}, use_global_device_ids=true, to_apply=%region_3.5 | all-reduce | flops 8192 | bytes 65536 | tf_op jit(solution)/shard_map/psum | solution.py:116
  (72 shorter events, 45.1 us)
Async XLA Ops:
  12.2 6.4 %collective-permute-start = (f32[48,2,1024]{2,0,1:T(8,128)}, f32[48,2,1024]{2,0,1:T(8,128)}, u32[]{:S(2)}, u32[]{:S(2)}) collective-permute-start(f32[48,2,1024]{2,0,1:T(8,128)} %get-tuple-element.81), channel_id=1, source_target_pairs={{0,4},{4,0},{8,12},{12,8},{16,20},{20,16},{24,28},{28,24},{1,5},{5... | collective-permute-start | bytes 1179656 | tf_op jit(solution)/shard_map/ppermute | solution.py:29
  12.6 12.8 %collective-permute-start.1 = (f32[48,2,1024]{2,0,1:T(8,128)}, f32[48,2,1024]{2,0,1:T(8,128)}, u32[]{:S(2)}, u32[]{:S(2)}) collective-permute-start(f32[48,2,1024]{2,0,1:T(8,128)} %get-tuple-element.80), channel_id=1, source_target_pairs={{0,8},{4,12},{8,0},{12,4},{16,24},{20,28},{24,16},{28,20},{1,9},{5... | collective-permute-start | bytes 1179656 | tf_op jit(solution)/shard_map/ppermute | solution.py:29
  15.1 18.3 %collective-permute-start.2 = (f32[48,2,1024]{2,0,1:T(8,128)}, f32[48,2,1024]{2,0,1:T(8,128)}, u32[]{:S(2)}, u32[]{:S(2)}) collective-permute-start(f32[48,2,1024]{2,0,1:T(8,128)} %get-tuple-element.79), channel_id=1, source_target_pairs={{0,12},{4,8},{8,4},{12,0},{16,28},{20,24},{24,20},{28,16},{1,13},{... | collective-permute-start | bytes 1179656 | tf_op jit(solution)/shard_map/ppermute | solution.py:29
  15.3 20.0 %collective-permute-start.3 = (f32[48,2,1024]{2,0,1:T(8,128)}, f32[48,2,1024]{2,0,1:T(8,128)}, u32[]{:S(2)}, u32[]{:S(2)}) collective-permute-start(f32[48,2,1024]{2,0,1:T(8,128)} %get-tuple-element.78), channel_id=1, source_target_pairs={{0,16},{4,20},{8,24},{12,28},{16,0},{20,4},{24,8},{28,12},{1,17},{... | collective-permute-start | bytes 1179656 | tf_op jit(solution)/shard_map/ppermute | solution.py:29
  17.0 34.4 %collective-permute-start.4 = (f32[48,2,1024]{2,0,1:T(8,128)}, f32[48,2,1024]{2,0,1:T(8,128)}, u32[]{:S(2)}, u32[]{:S(2)}) collective-permute-start(f32[48,2,1024]{2,0,1:T(8,128)} %get-tuple-element.77), channel_id=1, source_target_pairs={{0,20},{4,16},{8,28},{12,24},{16,4},{20,0},{24,12},{28,8},{1,21},{... | collective-permute-start | bytes 1179656 | tf_op jit(solution)/shard_map/ppermute | solution.py:29
  18.6 34.6 %collective-permute-start.5 = (f32[48,2,1024]{2,0,1:T(8,128)}, f32[48,2,1024]{2,0,1:T(8,128)S(1)}, u32[]{:S(2)}, u32[]{:S(2)}) collective-permute-start(f32[48,2,1024]{2,0,1:T(8,128)} %get-tuple-element.76), channel_id=1, source_target_pairs={{0,24},{4,28},{8,16},{12,20},{16,8},{20,12},{24,0},{28,4},{1,25},{... | collective-permute-start | bytes 1179656 | tf_op jit(solution)/shard_map/ppermute | solution.py:29
  25.4 28.6 %collective-permute-start.6 = (f32[48,2,1024]{2,0,1:T(8,128)S(1)}, f32[48,2,1024]{2,0,1:T(8,128)S(1)}, u32[]{:S(2)}, u32[]{:S(2)}) collective-permute-start(f32[48,2,1024]{2,0,1:T(8,128)S(1)} %get-tuple-element.75), channel_id=1, source_target_pairs={{0,28},{4,24},{8,20},{12,16},{16,12},{20,8},{24,4},{28,0},{1,29},{... | collective-permute-start | bytes 1179656 | tf_op jit(solution)/shard_map/ppermute | solution.py:29
  101.4 4.3 %copy-start.4 = (s32[16,256]{1,0:T(8,128)S(1)}, s32[16,256]{1,0:T(8,128)}, u32[]{:S(2)}) copy-start(s32[16,256]{1,0:T(8,128)} %param.11) | copy-start | bytes 49156
  101.4 4.3 %copy-start.5 = (f32[16,256]{1,0:T(8,128)S(1)}, f32[16,256]{1,0:T(8,128)}, u32[]{:S(2)}) copy-start(f32[16,256]{1,0:T(8,128)} %param.13) | copy-start | bytes 49156
  101.4 4.3 %copy-start.6 = (f32[16,256]{1,0:T(8,128)S(1)}, f32[16,256]{1,0:T(8,128)}, u32[]{:S(2)}) copy-start(f32[16,256]{1,0:T(8,128)} %param.14) | copy-start | bytes 49156
  101.4 4.3 %copy-start.3 = (s32[16,256]{1,0:T(8,128)S(1)}, s32[16,256]{1,0:T(8,128)}, u32[]{:S(2)}) copy-start(s32[16,256]{1,0:T(8,128)} %param.12) | copy-start | bytes 49156
  101.5 42.1 %all-to-all-start = ((f32[384,2,1024]{2,1,0:T(2,128)}), f32[384,2,1024]{2,1,0:T(2,128)S(1)}, u32[]{:S(2)}, u32[]{:S(2)}) async-start(f32[384,2,1024]{2,1,0:T(2,128)} %reshape_reshape.8), calls=%async_computation | async-start | bytes 6291456 | tf_op jit(solution)/shard_map/all_to_all | solution.py:94
  162.9 10.7 %collective-permute-start.7 = (f32[48,2,2,16,1]{0,3,4,2,1:T(8,128)S(1)}, f32[48,2,2,16,1]{0,3,4,2,1:T(8,128)S(1)}, u32[]{:S(2)}, u32[]{:S(2)}) collective-permute-start(f32[48,2,2,16,1]{0,3,4,2,1:T(8,128)S(1)} %copy.20), channel_id=1, source_target_pairs={{1,0},{2,1},{3,2},{5,4},{6,5},{7,6},{9,8},{10,9},{11,10},{13,12},{... | collective-permute-start | bytes 36872 | tf_op jit(solution)/shard_map/ppermute | solution.py:42
  166.4 9.6 %collective-permute-start.8 = (f32[48,2,2,16,1]{0,3,4,2,1:T(8,128)S(1)}, f32[48,2,2,16,1]{0,3,4,2,1:T(8,128)S(1)}, u32[]{:S(2)}, u32[]{:S(2)}) collective-permute-start(f32[48,2,2,16,1]{0,3,4,2,1:T(8,128)S(1)} %copy.22), channel_id=1, source_target_pairs={{0,1},{1,2},{2,3},{4,5},{5,6},{6,7},{8,9},{9,10},{10,11},{12,13},{... | collective-permute-start | bytes 36872 | tf_op jit(solution)/shard_map/ppermute | solution.py:41
  173.5 4.8 %copy-start.2 = (f32[48,2,2,16,255]{4,3,2,1,0:T(8,128)S(1)}, f32[48,2,2,16,255]{4,3,2,1,0:T(8,128)}, u32[]{:S(2)}) copy-start(f32[48,2,2,16,255]{4,3,2,1,0:T(8,128)} %get-tuple-element.73) | copy-start | bytes 9400324
  178.3 4.3 %copy-start = (f32[48,2,2,16,256]{4,3,2,1,0:T(8,128)S(1)}, f32[48,2,2,16,256]{4,3,2,1,0:T(8,128)}, u32[]{:S(2)}) copy-start(f32[48,2,2,16,256]{4,3,2,1,0:T(8,128)} %fusion.7) | copy-start | bytes 9437188
  178.3 4.7 %copy-start.1 = (f32[48,2,2,16,256]{4,3,2,1,0:T(8,128)S(1)}, f32[48,2,2,16,256]{4,3,2,1,0:T(8,128)}, u32[]{:S(2)}) copy-start(f32[48,2,2,16,256]{4,3,2,1,0:T(8,128)} %get-tuple-element.69) | copy-start | bytes 9437188
